TPU v7x, 32 devices: a whole 2x2x4 slice. The times are simulated.
32 devices in a mesh: gx: 8 (over y, x, core), gy: 4 (over z).
Axes of the slice: x: 2, y: 2, z: 4, core: 2. Of those that a mesh axis runs over, the one named last changes fastest.
Arguments:
- velocity: float32 [3, 128, 64, 512], P(None, 'gx', 'gy'), may hold values from -6 to 6
- stress: float32 [6, 128, 64, 512], P(None, 'gx', 'gy'), may hold values from -6 to 6
- pier_velocity: float32 [128, 16], P('gx', 'gy'), may hold values from -6 to 6
- buoyancy: float32 [128, 64, 512], P('gx', 'gy'), may hold values from 0.5 to 2
- layer: int32 [128], P('gx'), may hold values from 0 to 7, as said below
- lame_table: float32 [8], replicated, may hold values from 0.3 to 1.2
- shear_table: float32 [8], replicated, may hold values from 0.2 to 0.8
- relax_table: float32 [8], replicated, may hold values from 0.6 to 0.95
- impedance: float32 [16], P('gy'), may hold values from 0.5 to 2
- footprint: int32 [16, 16], replicated, may hold values from 0 to 32767, as said below
- damp_inverse: float32 [128, 128], replicated
Outputs:
- velocity_out: float32 [3, 128, 64, 512], P(None, 'gx', 'gy')
- stress_out: float32 [6, 128, 64, 512], P(None, 'gx', 'gy')
- pier_out: float32 [128, 16], P('gx', 'gy')
Inputs may be any that keep to these rules, and one draw needn't show every extreme that they name: `footprint`: row p lists the 16 cells of a square of 4 by 4 cells, row by row; squares may intersect and lie anywhere in the plane. `layer`: non-decreasing along depth; the first cell is in layer 0 and the last in layer 7.
All inputs are finite; a program needn't handle non-finite values.
Results may differ from a plain program's by a relative error of at most 0.00011.
Values sent between devices are 32-bit elements; how exact they have to be, the bound alone decides.
A program may use at most 192 MiB of HBM per device.

v0:
```python
import jax
import jax.numpy as jnp
from jax import lax
from jax.sharding import PartitionSpec as P

STEPS = 2
FOOT = 16
grid_ratio = 0.25
soil_gain = 0.2
pier_gain = 0.5


def extended(cells, sides, width):
    for axis, dim in sides:
        count = lax.axis_size(axis)
        ends = count - 1
        head = lax.slice_in_dim(cells, 0, width, axis=dim)
        tail = lax.slice_in_dim(cells, cells.shape[dim] - width, cells.shape[dim], axis=dim)
        cells = jnp.concatenate(
            [
                lax.ppermute(tail, axis, [(i, (i + 1) % count) for i in range(ends)]),
                cells,
                lax.ppermute(head, axis, [((i + 1) % count, i) for i in range(ends)]),
            ],
            axis=dim,
        )
    return cells


def forward_diff(padded, along):
    center = padded[1:-1, 1:-1, 1:-1]
    if along == 0:
        return padded[2:, 1:-1, 1:-1] - center
    if along == 1:
        return padded[1:-1, 2:, 1:-1] - center
    return padded[1:-1, 1:-1, 2:] - center


def backward_diff(padded, along):
    center = padded[1:-1, 1:-1, 1:-1]
    if along == 0:
        return center - padded[:-2, 1:-1, 1:-1]
    if along == 1:
        return center - padded[1:-1, :-2, 1:-1]
    return center - padded[1:-1, 1:-1, :-2]


def move_velocity(velocity, padded, buoyancy):
    scaled = grid_ratio * buoyancy
    first = velocity[0] + scaled * (
        backward_diff(padded[0], 2) + forward_diff(padded[3], 1) + forward_diff(padded[4], 0)
    )
    second = velocity[1] + scaled * (
        forward_diff(padded[3], 2) + backward_diff(padded[1], 1) + forward_diff(padded[5], 0)
    )
    third = velocity[2] + scaled * (
        forward_diff(padded[4], 2) + forward_diff(padded[5], 1) + backward_diff(padded[2], 0)
    )
    return jnp.stack([first, second, third])


def move_stress(stress, padded, lame_first, shear_mod, relax):
    strain_x = forward_diff(padded[0], 2)
    strain_y = forward_diff(padded[1], 1)
    strain_z = forward_diff(padded[2], 0)
    modulus = lame_first + 2.0 * shear_mod
    normal_x = relax * stress[0] + grid_ratio * (
        modulus * strain_x + lame_first * (strain_y + strain_z)
    )
    normal_y = relax * stress[1] + grid_ratio * (
        modulus * strain_y + lame_first * (strain_x + strain_z)
    )
    normal_z = relax * stress[2] + grid_ratio * (
        modulus * strain_z + lame_first * (strain_x + strain_y)
    )
    shear_xy = relax * stress[3] + grid_ratio * shear_mod * (
        backward_diff(padded[0], 1) + backward_diff(padded[1], 2)
    )
    shear_xz = relax * stress[4] + grid_ratio * shear_mod * (
        backward_diff(padded[0], 0) + backward_diff(padded[2], 2)
    )
    shear_yz = relax * stress[5] + grid_ratio * shear_mod * (
        backward_diff(padded[1], 0) + backward_diff(padded[2], 1)
    )
    return jnp.stack([normal_x, normal_y, normal_z, shear_xy, shear_xz, shear_yz])


def layer_values(layer, table):
    levels = jnp.arange(table.shape[0], dtype=jnp.int32)
    onehot = (layer[:, None] == levels[None, :]).astype(table.dtype)
    return jnp.sum(onehot * table[None, :], axis=1)[:, None, None]


def with_faces(fields):
    padded = extended(fields, (("gx", 1), ("gy", 2)), 1)
    return jnp.pad(padded, ((0, 0), (0, 0), (0, 0), (1, 1)))


def footprint_matches(cell_ids, footprint):
    piers = footprint.shape[0]
    equal = (cell_ids[:, None] == footprint.reshape(-1)[None, :]).astype(jnp.float32)
    return jnp.sum(equal.reshape(cell_ids.shape[0], piers, FOOT), axis=2)


def damp_columns(velocity, inverse):
    pencils = lax.all_to_all(velocity, "gx", split_axis=3, concat_axis=1, tiled=True)
    shape = pencils.shape
    flat = pencils.reshape(shape[0], shape[1], shape[2] * shape[3])
    damped = jnp.einsum("zk,fkm->fzm", inverse, flat, precision=lax.Precision.HIGHEST).reshape(
        shape
    )
    return lax.all_to_all(damped, "gx", split_axis=1, concat_axis=3, tiled=True)


def body(
    velocity,
    stress,
    pier_velocity,
    buoyancy,
    layer,
    lame_table,
    shear_table,
    relax_table,
    impedance,
    footprint,
    damp_inverse,
):
    depth_cells, side_cells, line_cells = (velocity.shape[1], velocity.shape[2], velocity.shape[3])
    own_piers = pier_velocity.shape[1]
    lame_first = layer_values(layer, lame_table)
    shear_mod = layer_values(layer, shear_table)
    relax = layer_values(layer, relax_table)
    row_start = lax.axis_index("gy") * side_cells
    cell_ids = row_start * line_cells + jnp.arange(side_cells * line_cells, dtype=jnp.int32)
    selector = footprint_matches(cell_ids, footprint)
    own_foot = lax.dynamic_slice_in_dim(footprint, lax.axis_index("gy") * own_piers, own_piers, 0)
    for time_step in range(STEPS):
        padded = with_faces(stress)
        velocity = move_velocity(velocity, padded, buoyancy)
        vertical = velocity[2].reshape(depth_cells, side_cells * line_cells)
        piece = lax.all_gather(velocity[2], "gy", axis=1, tiled=True)
        count = piece.shape[1]
        piece_ids = jnp.arange(count * line_cells, dtype=jnp.int32)
        picks = footprint_matches(piece_ids, own_foot)
        flat = piece.reshape(depth_cells, count * line_cells)
        summed = jnp.dot(
            flat, picks, precision=lax.Precision.HIGHEST, preferred_element_type=jnp.float32
        )
        mean_speed = summed / FOOT
        force = impedance[None, :] * (pier_velocity - mean_speed)
        pier_velocity = pier_velocity - pier_gain * force
        all_force = lax.all_gather(force, "gy", axis=1, tiled=True)
        pushed = jnp.dot(
            all_force,
            selector.T,
            precision=lax.Precision.HIGHEST,
            preferred_element_type=jnp.float32,
        )
        vertical = vertical + soil_gain * pushed
        velocity = jnp.stack(
            [velocity[0], velocity[1], vertical.reshape(depth_cells, side_cells, line_cells)]
        )
        velocity = damp_columns(velocity, damp_inverse)
        padded = with_faces(velocity)
        stress = move_stress(stress, padded, lame_first, shear_mod, relax)
    return (velocity, stress, pier_velocity)


def solution(mesh):
    placed = (
        P(None, "gx", "gy", None),
        P(None, "gx", "gy", None),
        P("gx", "gy"),
        P("gx", "gy", None),
        P("gx"),
        P(),
        P(),
        P(),
        P("gy"),
        P(),
        P(),
    )
    return jax.shard_map(
        body,
        mesh=mesh,
        in_specs=placed,
        out_specs=(P(None, "gx", "gy", None), P(None, "gx", "gy", None), P("gx", "gy")),
        check_vma=False,
    )
```

profile of v0, /device:TPU:11, one launch (start us, length us, event | category | flops | bytes accessed | tf_op | source)
XLA Modules:
  0.0 499.5 jit_solution(11973510932062096920)
XLA Ops:
  8.3 3.7 collective-permute-start
  14.6 2.3 constant_dynamic-update-slice_fusion.1
  16.9 3.0 collective-permute-done.1
  20.3 3.2 collective-permute-start.2
  25.6 2.9 collective-permute-done.2
  28.5 3.2 collective-permute-done.3
  31.7 4.2 select_maximum_fusion.4
  37.8 2.8 fusion.48
  40.9 2.9 convert_reduce_fusion.1
  45.5 2.3 copy.69
  47.9 5.0 fusion.58
  52.8 31.2 %all-gather.5.cloned.1.call-done = f32[16,64,512]{2,1,0:T(8,128)} async-done(((f32[16,16,512]{2,1,0:T(8,128)}), f32[16,64,512]{2,1,0:T(8,128)}) %all-gather.5.cloned.1.call-update) | async-done | bytes 2097168 | tf_op jit(solution)/shard_map/all_gather | solution.py:141
  84.0 2.9 copy.70
  86.9 2.6 fusion.7
  89.5 9.2 %all-gather = f32[4,4,16]{2,1,0:T(4,128)S(1)} all-gather(f32[1,4,16]{2,1,0:T(4,128)S(1)} %bitcast.214), channel_id=1, replica_groups=mesh['gx'=8,'gy'=4] {'gy'}, dimensions={0}, use_global_device_ids=true | all-gather | bytes 1280 | tf_op jit(solution)/shard_map/all_gather | solution.py:152
  99.9 8.8 %copy.50 = f32[3,16,16,512]{2,1,0,3:T(8,128)} copy(f32[3,16,16,512]{3,2,1,0:T(8,128)S(1)} %pad_maximum_fusion) | data formatting | bytes 3145728 | tf_op jit(solution)/shard_map/stack | solution.py:160
  108.7 8.9 %reshape.89 = f32[8,1,49152]{2,1,0:T(1,128)S(1)} reshape(f32[512,3,16,16]{3,2,1,0:T(8,128)} %bitcast.186) | data formatting | bytes 3145728
  117.5 26.2 %all_to_all.66 = f32[8,1,49152]{2,1,0:T(1,128)S(1)} all-to-all(f32[8,1,49152]{2,1,0:T(1,128)S(1)} %reshape.89), channel_id=1, replica_groups=mesh['gx'=8,'gy'=4] {'gx'}, dimensions={0} | all-to-all | bytes 3145728 | tf_op jit(solution)/shard_map/all_to_all | solution.py:106
  144.3 4.4 reduce
  148.8 8.7 %reshape.90 = f32[512,3,16,16]{3,2,1,0:T(8,128)} reshape(f32[8,49152]{1,0:T(8,128)S(1)} %reduce) | data formatting | bytes 3145728
  157.5 8.1 %copy.51 = f32[3,16,16,8,64]{4,2,1,3,0:T(8,128)S(1)} copy(f32[3,16,16,8,64]{2,1,0,4,3:T(8,128)} %bitcast.188) | data formatting | bytes 3145728 | tf_op jit(solution)/shard_map/all_to_all | solution.py:106
  167.4 5.2 %fusion.65 = f32[3,1024,128]{2,1,0:T(8,128)} fusion(f32[3,128,1024]{2,1,0:T(8,128)} %reshape.79, f32[128,128]{1,0:T(8,128)S(1)} %copy-done), kind=kOutput, calls=%fused_computation.160 | convolution fusion | flops 603979776 | bytes 3211264 | tf_op jit(solution)/shard_map/zk,fkm->fzm/dot_general | solution.py:109
  172.5 2.7 copy.53
  175.2 3.0 reshape.91
  178.2 24.5 %all_to_all.67 = f32[8,1,49152]{2,1,0:T(1,128)S(1)} all-to-all(f32[8,1,49152]{2,1,0:T(1,128)} %reshape.91), channel_id=1, replica_groups=mesh['gx'=8,'gy'=4] {'gx'}, dimensions={0} | all-to-all | bytes 3145728 | tf_op jit(solution)/shard_map/all_to_all | solution.py:112
  202.7 6.2 %reduce.1 = f32[8,49152]{1,0:T(8,128)} reduce(f32[8,1,49152]{2,1,0:T(1,128)S(1)} %all_to_all.67, f32[]{:T(128)} %broadcast.158), dimensions={1}, to_apply=%all_to_all.51.reduce_sub_computation | reduce | bytes 3145732 | tf_op jit(solution)/shard_map/all_to_all | solution.py:112
  208.9 2.7 reshape.92
  211.5 3.5 copy.56
  215.0 3.8 all_to_all.54
  219.8 3.6 collective-permute-start.4
  227.0 3.3 collective-permute-done.5
  230.5 3.8 collective-permute-start.6
  236.4 3.4 collective-permute-done.7
  253.2 3.2 collective-permute-start.8
  259.1 5.3 %collective-permute-done.9 = f32[6,1,16,512]{3,2,1,0:T(8,128)S(1)} collective-permute-done((f32[6,1,16,512]{3,2,1,0:T(8,128)S(1)}, f32[6,1,16,512]{3,2,1,0:T(8,128)S(1)}, u32[]{:S(2)}, u32[]{:S(2)}) %collective-permute-start.9) | collective-permute-done | bytes 196640 | tf_op jit(solution)/shard_map/ppermute | solution.py:23
  267.5 4.2 collective-permute-start.11
  275.0 2.3 squeeze.133
  277.3 5.8 %select_maximum_fusion = f32[6,18,18,514]{3,2,1,0:T(8,128)S(1)} fusion(f32[6,18,1,512]{3,2,1,0:T(1,128)} %collective-permute-done.11, f32[6,18,1,512]{3,2,1,0:T(1,128)} %collective-permute-done.10, f32[6,1,16,512]{3,2,1,0:T(8,128)} %copy-done.25, f32[6,16,16,512]{3,2,1,0:T(8,128)S(1)} %copy-done.2, f32[6,1,16,512]{3,2,1,0:T(8,128)S(1)} %collective-permute-done.8), kind=kLoop, calls=%fused_computation.9 | loop fusion | flops 11990592 | bytes 7978176 | tf_op jit(solution)/shard_map/concatenate | solution.py:19
  286.7 2.8 copy.55
  291.8 3.0 copy.57
  294.8 2.3 squeeze.130
  298.2 5.7 %fusion.35 = (f32[1,16,16,512]{3,2,1,0:T(8,128)S(1)}, f32[1,16,16,512]{3,2,1,0:T(8,128)}) fusion(f32[16,16,512]{2,1,0:T(8,128)} %squeeze.117, f32[18,18,514]{2,1,0:T(8,128)S(1)} %get-tuple-element.21, f32[18,18,514]{2,1,0:T(8,128)} %get-tuple-element.22, f32[18,18,514]{2,1,0:T(8,128)} %get-tuple-element.18, f32[16,16,512]{2,1,0:T(8,128)S(1)} %copy-done.5, ...), kind=kLoop, calls=%fused_computation.92 | loop fusion | flops 1966080 | bytes 8388608 | tf_op jit(solution)/shard_map/stack | solution.py:59
  303.9 24.7 %all-gather.7.cloned.1.call-done = f32[16,64,512]{2,1,0:T(8,128)} async-done(((f32[16,16,512]{2,1,0:T(8,128)}), f32[16,64,512]{2,1,0:T(8,128)}) %all-gather.7.cloned.1.call-update) | async-done | bytes 2097168 | tf_op jit(solution)/shard_map/all_gather | solution.py:141
  328.6 2.9 copy.73
  331.5 3.2 multiply_subtract_fusion
  334.7 9.2 %all-gather.1 = f32[4,4,16]{2,1,0:T(4,128)S(1)} all-gather(f32[1,4,16]{2,1,0:T(4,128)S(1)} %bitcast.215), channel_id=1, replica_groups=mesh['gx'=8,'gy'=4] {'gy'}, dimensions={0}, use_global_device_ids=true | all-gather | bytes 1280 | tf_op jit(solution)/shard_map/all_gather | solution.py:152
  345.1 8.8 %copy.59 = f32[3,16,16,512]{2,1,0,3:T(8,128)} copy(f32[3,16,16,512]{3,2,1,0:T(8,128)S(1)} %pad_maximum_fusion.1) | data formatting | bytes 3145728 | tf_op jit(solution)/shard_map/stack | solution.py:160
  353.9 8.9 %reshape.93 = f32[8,1,49152]{2,1,0:T(1,128)S(1)} reshape(f32[512,3,16,16]{3,2,1,0:T(8,128)} %bitcast.187) | data formatting | bytes 3145728
  362.7 26.4 %all_to_all.68 = f32[8,1,49152]{2,1,0:T(1,128)S(1)} all-to-all(f32[8,1,49152]{2,1,0:T(1,128)S(1)} %reshape.93), channel_id=1, replica_groups=mesh['gx'=8,'gy'=4] {'gx'}, dimensions={0} | all-to-all | bytes 3145728 | tf_op jit(solution)/shard_map/all_to_all | solution.py:106
  389.2 4.4 reduce.2
  393.6 8.7 %reshape.94 = f32[512,3,16,16]{3,2,1,0:T(8,128)} reshape(f32[8,49152]{1,0:T(8,128)S(1)} %reduce.2) | data formatting | bytes 3145728
  402.3 8.1 %copy.60 = f32[3,16,16,8,64]{4,2,1,3,0:T(8,128)S(1)} copy(f32[3,16,16,8,64]{2,1,0,4,3:T(8,128)} %bitcast.189) | data formatting | bytes 3145728 | tf_op jit(solution)/shard_map/all_to_all | solution.py:106
  412.2 5.2 %fusion.63 = f32[3,1024,128]{2,1,0:T(8,128)} fusion(f32[3,128,1024]{2,1,0:T(8,128)} %reshape.82, f32[128,128]{1,0:T(8,128)S(1)} %copy-done), kind=kOutput, calls=%fused_computation.158 | convolution fusion | flops 603979776 | bytes 3211264 | tf_op jit(solution)/shard_map/zk,fkm->fzm/dot_general | solution.py:109
  417.4 2.4 copy.62
  419.8 3.0 reshape.95
  422.8 24.5 %all_to_all.69 = f32[8,1,49152]{2,1,0:T(1,128)S(1)} all-to-all(f32[8,1,49152]{2,1,0:T(1,128)} %reshape.95), channel_id=1, replica_groups=mesh['gx'=8,'gy'=4] {'gx'}, dimensions={0} | all-to-all | bytes 3145728 | tf_op jit(solution)/shard_map/all_to_all | solution.py:112
  447.3 6.2 %reduce.3 = f32[8,49152]{1,0:T(8,128)} reduce(f32[8,1,49152]{2,1,0:T(1,128)S(1)} %all_to_all.69, f32[]{:T(128)} %broadcast.158), dimensions={1}, to_apply=%all_to_all.58.reduce_sub_computation | reduce | bytes 3145732 | tf_op jit(solution)/shard_map/all_to_all | solution.py:112
  453.5 2.7 reshape.96
  456.1 3.5 copy.64
  459.6 2.8 all_to_all.61
  462.5 3.6 collective-permute-start.12
  468.2 4.7 collective-permute-done.13
  473.1 3.8 collective-permute-start.14
  479.1 3.3 collective-permute-done.15
  (142 shorter events, 67.1 us)
Async XLA Ops:
  7.2 160.2 %copy-start = (f32[128,128]{1,0:T(8,128)S(1)}, f32[128,128]{1,0:T(8,128)}, u32[]{:S(2)}) copy-start(f32[128,128]{1,0:T(8,128)} %param.21) | copy-start | bytes 196612
  7.2 76.8 %all-gather.5.cloned.1.call-start = ((), (), s32[]{:S(2)}) async-start(), calls=%async_computation.4 | async-start | bytes 2621440 | tf_op jit(solution)/shard_map/all_gather | solution.py:141
  8.3 6.3 %collective-permute-start = (f32[6,1,16,512]{3,2,1,0:T(8,128)S(1)}, f32[6,1,16,512]{3,2,1,0:T(8,128)S(1)}, u32[]{:S(2)}, u32[]{:S(2)}) collective-permute-start(f32[6,1,16,512]{3,2,1,0:T(8,128)S(1)} %get-tuple-element.48), channel_id=1, source_target_pairs={{0,4},{4,8},{8,12},{12,16},{16,20},{20,24},{24,28},{1,5},{5,9},{9,... | collective-permute-start | bytes 589832 | tf_op jit(solution)/shard_map/ppermute | solution.py:21
  12.0 7.9 %collective-permute-start.1 = (f32[6,1,16,512]{3,2,1,0:T(8,128)S(1)}, f32[6,1,16,512]{3,2,1,0:T(8,128)S(1)}, u32[]{:S(2)}, u32[]{:S(2)}) collective-permute-start(f32[6,1,16,512]{3,2,1,0:T(8,128)S(1)} %get-tuple-element.47), channel_id=1, source_target_pairs={{4,0},{8,4},{12,8},{16,12},{20,16},{24,20},{28,24},{5,1},{9,5},{13... | collective-permute-start | bytes 589832 | tf_op jit(solution)/shard_map/ppermute | solution.py:23
  20.3 8.2 %collective-permute-start.2 = (f32[6,18,1,512]{3,2,1,0:T(1,128)S(1)}, f32[6,18,1,512]{3,2,1,0:T(1,128)S(1)}, u32[]{:S(2)}, u32[]{:S(2)}) collective-permute-start(f32[6,18,1,512]{3,2,1,0:T(1,128)S(1)} %get-tuple-element.32), channel_id=1, source_target_pairs={{0,1},{1,2},{2,3},{4,5},{5,6},{6,7},{8,9},{9,10},{10,11},{12,13},{... | collective-permute-start | bytes 663560 | tf_op jit(solution)/shard_map/ppermute | solution.py:21
  23.5 8.2 %collective-permute-start.3 = (f32[6,18,1,512]{3,2,1,0:T(1,128)S(1)}, f32[6,18,1,512]{3,2,1,0:T(1,128)S(1)}, u32[]{:S(2)}, u32[]{:S(2)}) collective-permute-start(f32[6,18,1,512]{3,2,1,0:T(1,128)S(1)} %get-tuple-element.33), channel_id=1, source_target_pairs={{1,0},{2,1},{3,2},{5,4},{6,5},{7,6},{9,8},{10,9},{11,10},{13,12},{... | collective-permute-start | bytes 663560 | tf_op jit(solution)/shard_map/ppermute | solution.py:23
  35.9 1.8 copy-start.4
  37.8 3.1 copy-start.27
  40.6 288.0 %all-gather.7.cloned.1.call-start = ((), (), s32[]{:S(2)}) async-start(), calls=%async_computation.5 | async-start | bytes 2621440 | tf_op jit(solution)/shard_map/all_gather | solution.py:141
  40.8 7.0 %copy-start.7 = (f32[18,18,514]{2,1,0:T(8,128)S(1)}, f32[18,18,514]{2,1,0:T(8,128)}, u32[]{:S(2)}) copy-start(f32[18,18,514]{2,1,0:T(8,128)} %get-tuple-element.28) | copy-start | bytes 1998436
  45.5 53.2 %copy-start.8 = (f32[8192,16]{0,1:T(8,128)}, f32[8192,16]{0,1:T(8,128)S(1)}, u32[]{:S(2)}) copy-start(f32[8192,16]{0,1:T(8,128)S(1)} %convert_reduce_fusion) | copy-start | bytes 1572868
  84.0 2.9 copy-start.11
  84.0 2.9 copy-start.28
  84.0 2.9 copy-start.29
  86.9 11.9 %copy-start.15 = (f32[2,8,16,512]{3,1,2,0:T(8,128)S(1)}, f32[2,8,16,512]{3,1,2,0:T(8,128)}, u32[]{:S(2)}) copy-start(f32[2,8,16,512]{3,1,2,0:T(8,128)} %copy.69) | copy-start | bytes 1572868
  86.9 12.8 %copy-start.17 = (f32[1,16,16,512]{3,2,1,0:T(8,128)S(1)}, f32[1,16,16,512]{3,2,1,0:T(8,128)}, u32[]{:S(2)}) copy-start(f32[1,16,16,512]{3,2,1,0:T(8,128)} %get-tuple-element.40) | copy-start | bytes 1572868
  86.9 12.8 %copy-start.18 = (f32[1,16,16,512]{3,2,1,0:T(8,128)S(1)}, f32[1,16,16,512]{3,2,1,0:T(8,128)}, u32[]{:S(2)}) copy-start(f32[1,16,16,512]{3,2,1,0:T(8,128)} %get-tuple-element.41) | copy-start | bytes 1572868
  215.0 8.3 %copy-start.30 = (f32[8]{0:T(128)S(1)}, f32[8]{0:T(128)}, u32[]{:S(2)}) copy-start(f32[8]{0:T(128)} %param.18) | copy-start | bytes 100
  215.0 8.3 %copy-start.31 = (s32[16]{0:T(128)S(1)}, s32[16]{0:T(128)}, u32[]{:S(2)}) copy-start(s32[16]{0:T(128)} %param.15) | copy-start | bytes 196
  215.0 8.3 %copy-start.32 = (f32[8]{0:T(128)S(1)}, f32[8]{0:T(128)}, u32[]{:S(2)}) copy-start(f32[8]{0:T(128)} %param.17) | copy-start | bytes 100
  215.0 8.3 %copy-start.33 = (f32[8]{0:T(128)S(1)}, f32[8]{0:T(128)}, u32[]{:S(2)}) copy-start(f32[8]{0:T(128)} %param.16) | copy-start | bytes 100
  219.8 5.6 %collective-permute-start.4 = (f32[3,1,16,512]{3,2,1,0:T(8,128)S(1)}, f32[3,1,16,512]{3,2,1,0:T(8,128)S(1)}, u32[]{:S(2)}, u32[]{:S(2)}) collective-permute-start(f32[3,1,16,512]{3,2,1,0:T(8,128)S(1)} %get-tuple-element.58), channel_id=1, source_target_pairs={{0,4},{4,8},{8,12},{12,16},{16,20},{20,24},{24,28},{1,5},{5,9},{9,... | collective-permute-start | bytes 294920 | tf_op jit(solution)/shard_map/ppermute | solution.py:21
  223.5 6.8 %collective-permute-start.5 = (f32[3,1,16,512]{3,2,1,0:T(8,128)S(1)}, f32[3,1,16,512]{3,2,1,0:T(8,128)S(1)}, u32[]{:S(2)}, u32[]{:S(2)}) collective-permute-start(f32[3,1,16,512]{3,2,1,0:T(8,128)S(1)} %get-tuple-element.57), channel_id=1, source_target_pairs={{4,0},{8,4},{12,8},{16,12},{20,16},{24,20},{28,24},{5,1},{9,5},{13... | collective-permute-start | bytes 294920 | tf_op jit(solution)/shard_map/ppermute | solution.py:23
  230.5 5.9 %collective-permute-start.6 = (f32[3,18,1,512]{3,2,1,0:T(1,128)S(1)}, f32[3,18,1,512]{3,2,1,0:T(1,128)S(1)}, u32[]{:S(2)}, u32[]{:S(2)}) collective-permute-start(f32[3,18,1,512]{3,2,1,0:T(1,128)S(1)} %get-tuple-element.51), channel_id=1, source_target_pairs={{0,1},{1,2},{2,3},{4,5},{5,6},{6,7},{8,9},{9,10},{10,11},{12,13},{... | collective-permute-start | bytes 331784 | tf_op jit(solution)/shard_map/ppermute | solution.py:21
  234.3 5.5 %collective-permute-start.7 = (f32[3,18,1,512]{3,2,1,0:T(1,128)S(1)}, f32[3,18,1,512]{3,2,1,0:T(1,128)S(1)}, u32[]{:S(2)}, u32[]{:S(2)}) collective-permute-start(f32[3,18,1,512]{3,2,1,0:T(1,128)S(1)} %get-tuple-element.52), channel_id=1, source_target_pairs={{1,0},{2,1},{3,2},{5,4},{6,5},{7,6},{9,8},{10,9},{11,10},{13,12},{... | collective-permute-start | bytes 331784 | tf_op jit(solution)/shard_map/ppermute | solution.py:23
  241.6 1.9 copy-start.3
  253.2 11.2 %copy-start.1 = (f32[6,16,16,512]{3,2,1,0:T(8,128)}, f32[6,16,16,512]{3,2,1,0:T(8,128)S(1)}, u32[]{:S(2)}) copy-start(f32[6,16,16,512]{3,2,1,0:T(8,128)S(1)} %get-tuple-element.6) | copy-start | bytes 9437188
  253.2 5.8 %collective-permute-start.8 = (f32[6,1,16,512]{3,2,1,0:T(8,128)S(1)}, f32[6,1,16,512]{3,2,1,0:T(8,128)S(1)}, u32[]{:S(2)}, u32[]{:S(2)}) collective-permute-start(f32[6,1,16,512]{3,2,1,0:T(8,128)S(1)} %get-tuple-element.45), channel_id=1, source_target_pairs={{0,4},{4,8},{8,12},{12,16},{16,20},{20,24},{24,28},{1,5},{5,9},{9,... | collective-permute-start | bytes 589832 | tf_op jit(solution)/shard_map/ppermute | solution.py:21
  256.5 7.9 %collective-permute-start.9 = (f32[6,1,16,512]{3,2,1,0:T(8,128)S(1)}, f32[6,1,16,512]{3,2,1,0:T(8,128)S(1)}, u32[]{:S(2)}, u32[]{:S(2)}) collective-permute-start(f32[6,1,16,512]{3,2,1,0:T(8,128)S(1)} %get-tuple-element.46), channel_id=1, source_target_pairs={{4,0},{8,4},{12,8},{16,12},{20,16},{24,20},{28,24},{5,1},{9,5},{13... | collective-permute-start | bytes 589832 | tf_op jit(solution)/shard_map/ppermute | solution.py:23
  264.4 7.4 %copy-start.25 = (f32[6,1,16,512]{3,2,1,0:T(8,128)}, f32[6,1,16,512]{3,2,1,0:T(8,128)S(1)}, u32[]{:S(2)}) copy-start(f32[6,1,16,512]{3,2,1,0:T(8,128)S(1)} %collective-permute-done.9) | copy-start | bytes 589828
  265.6 11.7 %collective-permute-start.10 = (f32[6,18,1,512]{3,2,1,0:T(1,128)}, f32[6,18,1,512]{3,2,1,0:T(1,128)}, u32[]{:S(2)}, u32[]{:S(2)}) collective-permute-start(f32[6,18,1,512]{3,2,1,0:T(1,128)} %get-tuple-element.30), channel_id=1, source_target_pairs={{0,1},{1,2},{2,3},{4,5},{5,6},{6,7},{8,9},{9,10},{10,11},{12,13},{... | collective-permute-start | bytes 663560 | tf_op jit(solution)/shard_map/ppermute | solution.py:21
  267.5 9.8 %collective-permute-start.11 = (f32[6,18,1,512]{3,2,1,0:T(1,128)}, f32[6,18,1,512]{3,2,1,0:T(1,128)}, u32[]{:S(2)}, u32[]{:S(2)}) collective-permute-start(f32[6,18,1,512]{3,2,1,0:T(1,128)} %get-tuple-element.31), channel_id=1, source_target_pairs={{1,0},{2,1},{3,2},{5,4},{6,5},{7,6},{9,8},{10,9},{11,10},{13,12},{... | collective-permute-start | bytes 663560 | tf_op jit(solution)/shard_map/ppermute | solution.py:23
  273.4 3.9 copy-start.2
  283.1 1.8 copy-start.5
  283.1 1.8 copy-start.13
  291.8 5.3 %copy-start.10 = (f32[16,16,512]{2,1,0:T(8,128)S(1)}, f32[16,16,512]{2,1,0:T(8,128)}, u32[]{:S(2)}) copy-start(f32[16,16,512]{2,1,0:T(8,128)} %fusion.25) | copy-start | bytes 1572868
  328.6 2.9 copy-start.12
  331.5 12.5 %copy-start.9 = (f32[8192,16]{0,1:T(8,128)S(1)}, f32[8192,16]{0,1:T(8,128)}, u32[]{:S(2)}) copy-start(f32[8192,16]{0,1:T(8,128)} %copy-done.8) | copy-start | bytes 1572868
  331.5 12.5 %copy-start.14 = (f32[2,8,16,512]{3,1,2,0:T(8,128)S(1)}, f32[2,8,16,512]{3,1,2,0:T(8,128)}, u32[]{:S(2)}) copy-start(f32[2,8,16,512]{3,1,2,0:T(8,128)} %copy.72) | copy-start | bytes 1572868
  331.5 13.4 %copy-start.16 = (f32[1,16,16,512]{3,2,1,0:T(8,128)S(1)}, f32[1,16,16,512]{3,2,1,0:T(8,128)}, u32[]{:S(2)}) copy-start(f32[1,16,16,512]{3,2,1,0:T(8,128)} %get-tuple-element.54) | copy-start | bytes 1572868
  462.5 10.7 %copy-start.6 = (f32[3,16,16,512]{3,2,1,0:T(8,128)}, f32[3,16,16,512]{3,2,1,0:T(8,128)S(1)}, u32[]{:S(2)}) copy-start(f32[3,16,16,512]{3,2,1,0:T(8,128)S(1)} %all_to_all.61) | copy-start | bytes 4718596
  462.5 5.5 %collective-permute-start.12 = (f32[3,1,16,512]{3,2,1,0:T(8,128)S(1)}, f32[3,1,16,512]{3,2,1,0:T(8,128)S(1)}, u32[]{:S(2)}, u32[]{:S(2)}) collective-permute-start(f32[3,1,16,512]{3,2,1,0:T(8,128)S(1)} %get-tuple-element.56), channel_id=1, source_target_pairs={{0,4},{4,8},{8,12},{12,16},{16,20},{20,24},{24,28},{1,5},{5,9},{9,... | collective-permute-start | bytes 294920 | tf_op jit(solution)/shard_map/ppermute | solution.py:21
  466.1 6.8 %collective-permute-start.13 = (f32[3,1,16,512]{3,2,1,0:T(8,128)S(1)}, f32[3,1,16,512]{3,2,1,0:T(8,128)S(1)}, u32[]{:S(2)}, u32[]{:S(2)}) collective-permute-start(f32[3,1,16,512]{3,2,1,0:T(8,128)S(1)} %get-tuple-element.55), channel_id=1, source_target_pairs={{4,0},{8,4},{12,8},{16,12},{20,16},{24,20},{28,24},{5,1},{9,5},{13... | collective-permute-start | bytes 294920 | tf_op jit(solution)/shard_map/ppermute | solution.py:23
  473.1 5.9 %collective-permute-start.14 = (f32[3,18,1,512]{3,2,1,0:T(1,128)S(1)}, f32[3,18,1,512]{3,2,1,0:T(1,128)S(1)}, u32[]{:S(2)}, u32[]{:S(2)}) collective-permute-start(f32[3,18,1,512]{3,2,1,0:T(1,128)S(1)} %get-tuple-element.49), channel_id=1, source_target_pairs={{0,1},{1,2},{2,3},{4,5},{5,6},{6,7},{8,9},{9,10},{10,11},{12,13},{... | collective-permute-start | bytes 331784 | tf_op jit(solution)/shard_map/ppermute | solution.py:21
  476.9 5.5 %collective-permute-start.15 = (f32[3,18,1,512]{3,2,1,0:T(1,128)S(1)}, f32[3,18,1,512]{3,2,1,0:T(1,128)S(1)}, u32[]{:S(2)}, u32[]{:S(2)}) collective-permute-start(f32[3,18,1,512]{3,2,1,0:T(1,128)S(1)} %get-tuple-element.50), channel_id=1, source_target_pairs={{1,0},{2,1},{3,2},{5,4},{6,5},{7,6},{9,8},{10,9},{11,10},{13,12},{... | collective-permute-start | bytes 331784 | tf_op jit(solution)/shard_map/ppermute | solution.py:23
  484.2 1.0 copy-start.23
  485.2 1.0 copy-start.24
  486.3 1.0 copy-start.20
  487.3 1.0 copy-start.21
  488.4 1.0 copy-start.22
  489.0 1.1 copy-start.19
  490.8 1.7 copy-start.26
Sparse Core Ops, SparseCore 0:
  40.7 43.2 all-gather.4
  286.8 41.7 all-gather.6
where the time goes:
time: 505 us; the launch traced here: 499 us
  local copies, waits for them, and re-layouts  145 us (29%)
  blocking collectives  120 us (24%)
  waiting for transfers between devices  86.1 us (17%)
  other arithmetic  70.9 us (14%)
  starting transfers between devices  45.2 us (9%)
  matrix products  17.4 us (3%)
  between operations  15.1 us (3%)
    unnamed x88, local copies, waits for them, and re-layouts  65.1 us
    all_gather x2, waiting for transfers between devices, body(): piece = lax.all_gather(velocity[2], 'gy', axis=1, tiled=True)  55.9 us
    all_to_all x2, blocking collectives, damp_columns(): lax.all_to_all(velocity, 'gx', split_axis=3, concat_axis=1, tiled=True)  52.6 us
    all_to_all x2, blocking collectives, damp_columns(): return lax.all_to_all(damped, 'gx', split_axis=1, concat_axis=3, tiled=True)  48.9 us
    ppermute x8, starting transfers between devices, extended(): lax.ppermute(tail, axis, [(i, (i + 1) % count) for i in range(ends)])  26.7 us
    ppermute x8, waiting for transfers between devices, extended(): lax.ppermute(head, axis, [((i + 1) % count, i) for i in range(ends)])  26.2 us
    all_gather x2, blocking collectives, body(): all_force = lax.all_gather(force, 'gy', axis=1, tiled=True)  18.4 us
    ppermute x8, starting transfers between devices, extended(): lax.ppermute(head, axis, [((i + 1) % count, i) for i in range(ends)])  18.2 us
  transfers between devices with their start and end apart: 18, of which 12 were waited for; matrix products, arithmetic and copies ran while one was open for 8% of the time, Pallas kernels for 0%

commit v1 on v0

--- a/solution.py
+++ b/solution.py
@@ -103,7 +103,10 @@
 
 
 def damp_columns(velocity, inverse):
-    pencils = lax.all_to_all(velocity, "gx", split_axis=3, concat_axis=1, tiled=True)
+    size = lax.axis_size("gx")
+    blocks = jnp.stack(jnp.split(velocity, size, axis=3), axis=0)
+    blocks = lax.all_to_all(blocks, "gx", split_axis=0, concat_axis=0)
+    pencils = jnp.concatenate(blocks, axis=1)
     shape = pencils.shape
     flat = pencils.reshape(shape[0], shape[1], shape[2] * shape[3])
     damped = jnp.einsum("zk,fkm->fzm", inverse, flat, precision=lax.Precision.HIGHEST).reshape(

time: 505 us -> 469 us (0.929)
  local copies, waits for them, and re-layouts: 145 us -> 108 us
    all_to_all x3 -> x1, local copies, waits for them, and re-layouts: 16.8 us -> 0.52 us  [damp_columns(): blocks = lax.all_to_all(blocks, 'gx', split_axis=0, concat_axis=0)]
    unnamed x88 -> x102, local copies, waits for them, and re-layouts: 65.1 us -> 54.3 us
    another operation x2 -> x4, local copies, waits for them, and re-layouts: 17.6 us -> 7.57 us  [the longest x2 5.74 us: damp_columns(): flat = pencils.reshape(shape[0], shape[1], shape[2] * shape[3])]
where the time goes in v1:
time: 469 us; the launch traced here: 463 us
  blocking collectives  120 us (26%)
  local copies, waits for them, and re-layouts  108 us (23%)
  waiting for transfers between devices  85.7 us (18%)
  other arithmetic  74.2 us (16%)
  starting transfers between devices  45.7 us (10%)
  between operations  15.1 us (3%)
  matrix products  14.6 us (3%)
    all_gather x2, waiting for transfers between devices, body(): piece = lax.all_gather(velocity[2], 'gy', axis=1, tiled=True)  55.6 us
    unnamed x102, local copies, waits for them, and re-layouts  54.3 us
    all_to_all x2, blocking collectives, damp_columns(): blocks = lax.all_to_all(blocks, 'gx', split_axis=0, concat_axis=0)  52.2 us
    all_to_all x2, blocking collectives, damp_columns(): return lax.all_to_all(damped, 'gx', split_axis=1, concat_axis=3, tiled=True)  49.6 us
    ppermute x8, starting transfers between devices, extended(): lax.ppermute(tail, axis, [(i, (i + 1) % count) for i in range(ends)])  26.7 us
    ppermute x8, waiting for transfers between devices, extended(): lax.ppermute(head, axis, [((i + 1) % count, i) for i in range(ends)])  26 us
    all_gather x2, blocking collectives, body(): all_force = lax.all_gather(force, 'gy', axis=1, tiled=True)  18.6 us
    ppermute x8, starting transfers between devices, extended(): lax.ppermute(head, axis, [((i + 1) % count, i) for i in range(ends)])  18.4 us
  transfers between devices with their start and end apart: 18, of which 12 were waited for; matrix products, arithmetic and copies ran while one was open for 8% of the time, Pallas kernels for 0%

profile of v1, /device:TPU:11, one launch (start us, length us, event | category | flops | bytes accessed | tf_op | source)
XLA Modules:
  0.0 463.2 jit_solution(16718585672030012925)
XLA Ops:
  8.3 3.7 collective-permute-start
  14.6 2.3 constant_dynamic-update-slice_fusion.1
  16.9 3.0 collective-permute-done.1
  20.3 3.2 collective-permute-start.2
  25.6 2.9 collective-permute-done.2
  28.5 3.2 collective-permute-done.3
  31.7 4.2 select_maximum_fusion.4
  37.8 2.8 fusion.48
  41.2 2.9 convert_reduce_fusion.1
  45.9 2.4 copy.65
  48.2 4.9 %fusion.58 = (f32[1,16,16,512]{3,2,1,0:T(8,128)}, f32[1,16,16,512]{3,2,1,0:T(8,128)}) fusion(f32[18,18,514]{2,1,0:T(8,128)S(1)} %get-tuple-element.27, f32[18,18,514]{2,1,0:T(8,128)S(1)} %copy-done.7, f32[18,18,514]{2,1,0:T(8,128)} %get-tuple-element.24, f32[3,16,16,512]{3,2,1,0:T(8,128)} %param.11, f32[16,16,512]{2,1,0:T(8,128)S(1)} %copy-done.4, ...), kind=kLoop, calls=%fused_computation.133 | loop fusion | flops 1966080 | bytes 8388608 | tf_op jit(solution)/shard_map/stack | solution.py:59
  53.2 30.8 %all-gather.5.cloned.1.call-done = f32[16,64,512]{2,1,0:T(8,128)} async-done(((f32[16,16,512]{2,1,0:T(8,128)}), f32[16,64,512]{2,1,0:T(8,128)}) %all-gather.5.cloned.1.call-update) | async-done | bytes 2097168 | tf_op jit(solution)/shard_map/all_gather | solution.py:144
  84.0 2.9 copy.66
  86.9 2.6 fusion.7
  89.5 9.2 %all-gather = f32[4,4,16]{2,1,0:T(4,128)S(1)} all-gather(f32[1,4,16]{2,1,0:T(4,128)S(1)} %bitcast.268), channel_id=1, replica_groups=mesh['gx'=8,'gy'=4] {'gy'}, dimensions={0}, use_global_device_ids=true | all-gather | bytes 1280 | tf_op jit(solution)/shard_map/all_gather | solution.py:155
  106.8 3.8 reshape.87
  110.6 26.2 %all_to_all.46 = f32[8,1,49152]{2,1,0:T(1,128)S(1)} all-to-all(f32[8,1,49152]{2,1,0:T(1,128)S(1)} %reshape.87), channel_id=1, replica_groups=mesh['gx'=8,'gy'=4] {'gx'}, dimensions={0} | all-to-all | bytes 3145728 | tf_op jit(solution)/shard_map/all_to_all | solution.py:108
  137.3 6.1 %reduce = f32[8,49152]{1,0:T(8,128)} reduce(f32[8,1,49152]{2,1,0:T(1,128)S(1)} %all_to_all.46, f32[]{:T(128)} %broadcast.158), dimensions={1}, to_apply=%all_to_all.32.reduce_sub_computation | reduce | bytes 3145732 | tf_op jit(solution)/shard_map/all_to_all | solution.py:108
  143.4 2.7 reshape.88
  148.0 2.9 reshape_reshape.6
  150.9 3.8 fusion.81
  154.7 2.3 copy.50
  157.0 3.0 reshape.89
  160.0 24.7 %all_to_all.47 = f32[8,1,49152]{2,1,0:T(1,128)S(1)} all-to-all(f32[8,1,49152]{2,1,0:T(1,128)} %reshape.89), channel_id=1, replica_groups=mesh['gx'=8,'gy'=4] {'gx'}, dimensions={0} | all-to-all | bytes 3145728 | tf_op jit(solution)/shard_map/all_to_all | solution.py:115
  184.7 6.1 %reduce.1 = f32[8,49152]{1,0:T(8,128)} reduce(f32[8,1,49152]{2,1,0:T(1,128)S(1)} %all_to_all.47, f32[]{:T(128)} %broadcast.158), dimensions={1}, to_apply=%all_to_all.33.reduce_sub_computation | reduce | bytes 3145732 | tf_op jit(solution)/shard_map/all_to_all | solution.py:115
  190.8 2.7 reshape.90
  193.5 3.5 copy.53
  197.0 3.8 all_to_all.36
  201.7 3.5 collective-permute-start.4
  208.9 3.3 collective-permute-done.5
  212.4 3.8 collective-permute-start.6
  216.2 2.3 collective-permute-start.7
  218.6 3.1 collective-permute-done.7
  235.3 3.2 collective-permute-start.8
  241.1 5.3 %collective-permute-done.9 = f32[6,1,16,512]{3,2,1,0:T(8,128)S(1)} collective-permute-done((f32[6,1,16,512]{3,2,1,0:T(8,128)S(1)}, f32[6,1,16,512]{3,2,1,0:T(8,128)S(1)}, u32[]{:S(2)}, u32[]{:S(2)}) %collective-permute-start.9) | collective-permute-done | bytes 196640 | tf_op jit(solution)/shard_map/ppermute | solution.py:23
  249.6 4.2 collective-permute-start.11
  257.0 2.3 squeeze.133
  259.3 5.8 %select_maximum_fusion = f32[6,18,18,514]{3,2,1,0:T(8,128)S(1)} fusion(f32[6,18,1,512]{3,2,1,0:T(1,128)} %collective-permute-done.11, f32[6,18,1,512]{3,2,1,0:T(1,128)} %collective-permute-done.10, f32[6,1,16,512]{3,2,1,0:T(8,128)} %copy-done.25, f32[6,16,16,512]{3,2,1,0:T(8,128)S(1)} %copy-done.2, f32[6,1,16,512]{3,2,1,0:T(8,128)S(1)} %collective-permute-done.8), kind=kLoop, calls=%fused_computation.9 | loop fusion | flops 11990592 | bytes 7978176 | tf_op jit(solution)/shard_map/concatenate | solution.py:19
  268.7 2.8 copy.52
  271.5 2.3 squeeze.117
  273.9 2.9 copy.54
  276.8 2.3 squeeze.130
  280.2 5.6 %fusion.35 = (f32[1,16,16,512]{3,2,1,0:T(8,128)S(1)}, f32[1,16,16,512]{3,2,1,0:T(8,128)}) fusion(f32[16,16,512]{2,1,0:T(8,128)} %squeeze.117, f32[18,18,514]{2,1,0:T(8,128)S(1)} %get-tuple-element.21, f32[18,18,514]{2,1,0:T(8,128)} %get-tuple-element.22, f32[18,18,514]{2,1,0:T(8,128)} %get-tuple-element.18, f32[16,16,512]{2,1,0:T(8,128)S(1)} %copy-done.5, ...), kind=kLoop, calls=%fused_computation.92 | loop fusion | flops 1966080 | bytes 8388608 | tf_op jit(solution)/shard_map/stack | solution.py:59
  285.8 24.8 %all-gather.7.cloned.1.call-done = f32[16,64,512]{2,1,0:T(8,128)} async-done(((f32[16,16,512]{2,1,0:T(8,128)}), f32[16,64,512]{2,1,0:T(8,128)}) %all-gather.7.cloned.1.call-update) | async-done | bytes 2097168 | tf_op jit(solution)/shard_map/all_gather | solution.py:144
  310.6 2.9 copy.69
  313.5 3.3 multiply_subtract_fusion
  316.8 9.4 %all-gather.1 = f32[4,4,16]{2,1,0:T(4,128)S(1)} all-gather(f32[1,4,16]{2,1,0:T(4,128)S(1)} %bitcast.269), channel_id=1, replica_groups=mesh['gx'=8,'gy'=4] {'gy'}, dimensions={0}, use_global_device_ids=true | all-gather | bytes 1280 | tf_op jit(solution)/shard_map/all_gather | solution.py:155
  334.2 3.8 reshape.91
  338.0 26.0 %all_to_all.48 = f32[8,1,49152]{2,1,0:T(1,128)S(1)} all-to-all(f32[8,1,49152]{2,1,0:T(1,128)S(1)} %reshape.91), channel_id=1, replica_groups=mesh['gx'=8,'gy'=4] {'gx'}, dimensions={0} | all-to-all | bytes 3145728 | tf_op jit(solution)/shard_map/all_to_all | solution.py:108
  364.0 6.1 %reduce.2 = f32[8,49152]{1,0:T(8,128)} reduce(f32[8,1,49152]{2,1,0:T(1,128)S(1)} %all_to_all.48, f32[]{:T(128)} %broadcast.158), dimensions={1}, to_apply=%all_to_all.37.reduce_sub_computation | reduce | bytes 3145732 | tf_op jit(solution)/shard_map/all_to_all | solution.py:108
  370.2 2.7 reshape.92
  374.8 2.9 reshape_reshape.7
  377.6 3.8 fusion.79
  381.4 2.3 copy.58
  383.7 3.0 reshape.93
  386.7 24.9 %all_to_all.49 = f32[8,1,49152]{2,1,0:T(1,128)S(1)} all-to-all(f32[8,1,49152]{2,1,0:T(1,128)} %reshape.93), channel_id=1, replica_groups=mesh['gx'=8,'gy'=4] {'gx'}, dimensions={0} | all-to-all | bytes 3145728 | tf_op jit(solution)/shard_map/all_to_all | solution.py:115
  411.6 6.1 %reduce.3 = f32[8,49152]{1,0:T(8,128)} reduce(f32[8,1,49152]{2,1,0:T(1,128)S(1)} %all_to_all.49, f32[]{:T(128)} %broadcast.158), dimensions={1}, to_apply=%all_to_all.38.reduce_sub_computation | reduce | bytes 3145732 | tf_op jit(solution)/shard_map/all_to_all | solution.py:115
  417.7 2.7 reshape.94
  420.4 3.5 copy.60
  423.9 2.8 all_to_all.41
  426.8 3.5 collective-permute-start.12
  432.4 4.7 %collective-permute-done.13 = f32[3,1,16,512]{3,2,1,0:T(8,128)S(1)} collective-permute-done((f32[3,1,16,512]{3,2,1,0:T(8,128)S(1)}, f32[3,1,16,512]{3,2,1,0:T(8,128)S(1)}, u32[]{:S(2)}, u32[]{:S(2)}) %collective-permute-start.13) | collective-permute-done | bytes 98336 | tf_op jit(solution)/shard_map/ppermute | solution.py:23
  437.4 3.8 collective-permute-start.14
  443.3 3.4 collective-permute-done.15
  (156 shorter events, 76.5 us)
Async XLA Ops:
  7.2 143.7 %copy-start = (f32[128,128]{1,0:T(8,128)S(1)}, f32[128,128]{1,0:T(8,128)}, u32[]{:S(2)}) copy-start(f32[128,128]{1,0:T(8,128)} %param.21) | copy-start | bytes 196612
  7.2 76.8 %all-gather.5.cloned.1.call-start = ((), (), s32[]{:S(2)}) async-start(), calls=%async_computation.4 | async-start | bytes 2621440 | tf_op jit(solution)/shard_map/all_gather | solution.py:144
  8.3 6.3 %collective-permute-start = (f32[6,1,16,512]{3,2,1,0:T(8,128)S(1)}, f32[6,1,16,512]{3,2,1,0:T(8,128)S(1)}, u32[]{:S(2)}, u32[]{:S(2)}) collective-permute-start(f32[6,1,16,512]{3,2,1,0:T(8,128)S(1)} %get-tuple-element.48), channel_id=1, source_target_pairs={{0,4},{4,8},{8,12},{12,16},{16,20},{20,24},{24,28},{1,5},{5,9},{9,... | collective-permute-start | bytes 589832 | tf_op jit(solution)/shard_map/ppermute | solution.py:21
  12.0 7.9 %collective-permute-start.1 = (f32[6,1,16,512]{3,2,1,0:T(8,128)S(1)}, f32[6,1,16,512]{3,2,1,0:T(8,128)S(1)}, u32[]{:S(2)}, u32[]{:S(2)}) collective-permute-start(f32[6,1,16,512]{3,2,1,0:T(8,128)S(1)} %get-tuple-element.47), channel_id=1, source_target_pairs={{4,0},{8,4},{12,8},{16,12},{20,16},{24,20},{28,24},{5,1},{9,5},{13... | collective-permute-start | bytes 589832 | tf_op jit(solution)/shard_map/ppermute | solution.py:23
  20.3 8.2 %collective-permute-start.2 = (f32[6,18,1,512]{3,2,1,0:T(1,128)S(1)}, f32[6,18,1,512]{3,2,1,0:T(1,128)S(1)}, u32[]{:S(2)}, u32[]{:S(2)}) collective-permute-start(f32[6,18,1,512]{3,2,1,0:T(1,128)S(1)} %get-tuple-element.32), channel_id=1, source_target_pairs={{0,1},{1,2},{2,3},{4,5},{5,6},{6,7},{8,9},{9,10},{10,11},{12,13},{... | collective-permute-start | bytes 663560 | tf_op jit(solution)/shard_map/ppermute | solution.py:21
  23.5 8.2 %collective-permute-start.3 = (f32[6,18,1,512]{3,2,1,0:T(1,128)S(1)}, f32[6,18,1,512]{3,2,1,0:T(1,128)S(1)}, u32[]{:S(2)}, u32[]{:S(2)}) collective-permute-start(f32[6,18,1,512]{3,2,1,0:T(1,128)S(1)} %get-tuple-element.33), channel_id=1, source_target_pairs={{1,0},{2,1},{3,2},{5,4},{6,5},{7,6},{9,8},{10,9},{11,10},{13,12},{... | collective-permute-start | bytes 663560 | tf_op jit(solution)/shard_map/ppermute | solution.py:23
  35.9 1.8 copy-start.4
  37.8 3.4 copy-start.27
  40.6 270.0 %all-gather.7.cloned.1.call-start = ((), (), s32[]{:S(2)}) async-start(), calls=%async_computation.5 | async-start | bytes 2621440 | tf_op jit(solution)/shard_map/all_gather | solution.py:144
  41.2 7.0 %copy-start.7 = (f32[18,18,514]{2,1,0:T(8,128)S(1)}, f32[18,18,514]{2,1,0:T(8,128)}, u32[]{:S(2)}) copy-start(f32[18,18,514]{2,1,0:T(8,128)} %get-tuple-element.28) | copy-start | bytes 1998436
  45.8 52.9 %copy-start.8 = (f32[8192,16]{0,1:T(8,128)}, f32[8192,16]{0,1:T(8,128)S(1)}, u32[]{:S(2)}) copy-start(f32[8192,16]{0,1:T(8,128)S(1)} %convert_reduce_fusion) | copy-start | bytes 1572868
  53.1 33.7 %copy-start.11 = (f32[32768,4]{0,1:T(4,128)S(1)}, f32[32768,4]{0,1:T(4,128)}, u32[]{:S(2)}) copy-start(f32[32768,4]{0,1:T(4,128)} %convert_reduce_fusion.1) | copy-start | bytes 1572868
  53.2 33.7 %copy-start.28 = (f32[16,4]{0,1:T(4,128)S(1)}, f32[16,4]{0,1:T(4,128)}, u32[]{:S(2)}) copy-start(f32[16,4]{0,1:T(4,128)} %param.13) | copy-start | bytes 772
  53.2 33.7 %copy-start.29 = (f32[4]{0:T(128)S(1)}, f32[4]{0:T(128)}, u32[]{:S(2)}) copy-start(f32[4]{0:T(128)} %param.19) | copy-start | bytes 52
  84.0 14.7 %copy-start.15 = (f32[2,8,16,512]{3,1,2,0:T(8,128)S(1)}, f32[2,8,16,512]{3,1,2,0:T(8,128)}, u32[]{:S(2)}) copy-start(f32[2,8,16,512]{3,1,2,0:T(8,128)} %copy.65) | copy-start | bytes 1572868
  86.8 12.8 %copy-start.17 = (f32[1,16,16,512]{3,2,1,0:T(8,128)S(1)}, f32[1,16,16,512]{3,2,1,0:T(8,128)}, u32[]{:S(2)}) copy-start(f32[1,16,16,512]{3,2,1,0:T(8,128)} %get-tuple-element.40) | copy-start | bytes 1572868
  86.9 12.8 %copy-start.18 = (f32[1,16,16,512]{3,2,1,0:T(8,128)S(1)}, f32[1,16,16,512]{3,2,1,0:T(8,128)}, u32[]{:S(2)}) copy-start(f32[1,16,16,512]{3,2,1,0:T(8,128)} %get-tuple-element.41) | copy-start | bytes 1572868
  197.0 8.3 %copy-start.30 = (f32[8]{0:T(128)S(1)}, f32[8]{0:T(128)}, u32[]{:S(2)}) copy-start(f32[8]{0:T(128)} %param.18) | copy-start | bytes 100
  197.0 8.3 %copy-start.31 = (s32[16]{0:T(128)S(1)}, s32[16]{0:T(128)}, u32[]{:S(2)}) copy-start(s32[16]{0:T(128)} %param.15) | copy-start | bytes 196
  197.0 8.3 %copy-start.32 = (f32[8]{0:T(128)S(1)}, f32[8]{0:T(128)}, u32[]{:S(2)}) copy-start(f32[8]{0:T(128)} %param.17) | copy-start | bytes 100
  197.0 8.3 %copy-start.33 = (f32[8]{0:T(128)S(1)}, f32[8]{0:T(128)}, u32[]{:S(2)}) copy-start(f32[8]{0:T(128)} %param.16) | copy-start | bytes 100
  201.7 5.6 %collective-permute-start.4 = (f32[3,1,16,512]{3,2,1,0:T(8,128)S(1)}, f32[3,1,16,512]{3,2,1,0:T(8,128)S(1)}, u32[]{:S(2)}, u32[]{:S(2)}) collective-permute-start(f32[3,1,16,512]{3,2,1,0:T(8,128)S(1)} %get-tuple-element.58), channel_id=1, source_target_pairs={{0,4},{4,8},{8,12},{12,16},{16,20},{20,24},{24,28},{1,5},{5,9},{9,... | collective-permute-start | bytes 294920 | tf_op jit(solution)/shard_map/ppermute | solution.py:21
  205.4 6.8 %collective-permute-start.5 = (f32[3,1,16,512]{3,2,1,0:T(8,128)S(1)}, f32[3,1,16,512]{3,2,1,0:T(8,128)S(1)}, u32[]{:S(2)}, u32[]{:S(2)}) collective-permute-start(f32[3,1,16,512]{3,2,1,0:T(8,128)S(1)} %get-tuple-element.57), channel_id=1, source_target_pairs={{4,0},{8,4},{12,8},{16,12},{20,16},{24,20},{28,24},{5,1},{9,5},{13... | collective-permute-start | bytes 294920 | tf_op jit(solution)/shard_map/ppermute | solution.py:23
  212.4 6.1 %collective-permute-start.6 = (f32[3,18,1,512]{3,2,1,0:T(1,128)S(1)}, f32[3,18,1,512]{3,2,1,0:T(1,128)S(1)}, u32[]{:S(2)}, u32[]{:S(2)}) collective-permute-start(f32[3,18,1,512]{3,2,1,0:T(1,128)S(1)} %get-tuple-element.51), channel_id=1, source_target_pairs={{0,1},{1,2},{2,3},{4,5},{5,6},{6,7},{8,9},{9,10},{10,11},{12,13},{... | collective-permute-start | bytes 331784 | tf_op jit(solution)/shard_map/ppermute | solution.py:21
  216.2 5.5 %collective-permute-start.7 = (f32[3,18,1,512]{3,2,1,0:T(1,128)S(1)}, f32[3,18,1,512]{3,2,1,0:T(1,128)S(1)}, u32[]{:S(2)}, u32[]{:S(2)}) collective-permute-start(f32[3,18,1,512]{3,2,1,0:T(1,128)S(1)} %get-tuple-element.52), channel_id=1, source_target_pairs={{1,0},{2,1},{3,2},{5,4},{6,5},{7,6},{9,8},{10,9},{11,10},{13,12},{... | collective-permute-start | bytes 331784 | tf_op jit(solution)/shard_map/ppermute | solution.py:23
  223.5 1.9 copy-start.3
  235.2 11.2 %copy-start.1 = (f32[6,16,16,512]{3,2,1,0:T(8,128)}, f32[6,16,16,512]{3,2,1,0:T(8,128)S(1)}, u32[]{:S(2)}) copy-start(f32[6,16,16,512]{3,2,1,0:T(8,128)S(1)} %get-tuple-element.6) | copy-start | bytes 9437188
  235.3 5.8 %collective-permute-start.8 = (f32[6,1,16,512]{3,2,1,0:T(8,128)S(1)}, f32[6,1,16,512]{3,2,1,0:T(8,128)S(1)}, u32[]{:S(2)}, u32[]{:S(2)}) collective-permute-start(f32[6,1,16,512]{3,2,1,0:T(8,128)S(1)} %get-tuple-element.45), channel_id=1, source_target_pairs={{0,4},{4,8},{8,12},{12,16},{16,20},{20,24},{24,28},{1,5},{5,9},{9,... | collective-permute-start | bytes 589832 | tf_op jit(solution)/shard_map/ppermute | solution.py:21
  238.5 7.9 %collective-permute-start.9 = (f32[6,1,16,512]{3,2,1,0:T(8,128)S(1)}, f32[6,1,16,512]{3,2,1,0:T(8,128)S(1)}, u32[]{:S(2)}, u32[]{:S(2)}) collective-permute-start(f32[6,1,16,512]{3,2,1,0:T(8,128)S(1)} %get-tuple-element.46), channel_id=1, source_target_pairs={{4,0},{8,4},{12,8},{16,12},{20,16},{24,20},{28,24},{5,1},{9,5},{13... | collective-permute-start | bytes 589832 | tf_op jit(solution)/shard_map/ppermute | solution.py:23
  246.4 9.0 %copy-start.25 = (f32[6,1,16,512]{3,2,1,0:T(8,128)}, f32[6,1,16,512]{3,2,1,0:T(8,128)S(1)}, u32[]{:S(2)}) copy-start(f32[6,1,16,512]{3,2,1,0:T(8,128)S(1)} %collective-permute-done.9) | copy-start | bytes 589828
  247.6 11.7 %collective-permute-start.10 = (f32[6,18,1,512]{3,2,1,0:T(1,128)}, f32[6,18,1,512]{3,2,1,0:T(1,128)}, u32[]{:S(2)}, u32[]{:S(2)}) collective-permute-start(f32[6,18,1,512]{3,2,1,0:T(1,128)} %get-tuple-element.30), channel_id=1, source_target_pairs={{0,1},{1,2},{2,3},{4,5},{5,6},{6,7},{8,9},{9,10},{10,11},{12,13},{... | collective-permute-start | bytes 663560 | tf_op jit(solution)/shard_map/ppermute | solution.py:21
  249.6 9.8 %collective-permute-start.11 = (f32[6,18,1,512]{3,2,1,0:T(1,128)}, f32[6,18,1,512]{3,2,1,0:T(1,128)}, u32[]{:S(2)}, u32[]{:S(2)}) collective-permute-start(f32[6,18,1,512]{3,2,1,0:T(1,128)} %get-tuple-element.31), channel_id=1, source_target_pairs={{1,0},{2,1},{3,2},{5,4},{6,5},{7,6},{9,8},{10,9},{11,10},{13,12},{... | collective-permute-start | bytes 663560 | tf_op jit(solution)/shard_map/ppermute | solution.py:23
  255.4 3.9 copy-start.2
  265.1 1.8 copy-start.5
  265.1 1.8 copy-start.13
  271.5 7.5 %copy-start.10 = (f32[16,16,512]{2,1,0:T(8,128)S(1)}, f32[16,16,512]{2,1,0:T(8,128)}, u32[]{:S(2)}) copy-start(f32[16,16,512]{2,1,0:T(8,128)} %fusion.25) | copy-start | bytes 1572868
  285.8 27.7 %copy-start.12 = (f32[32768,4]{0,1:T(4,128)S(1)}, f32[32768,4]{0,1:T(4,128)}, u32[]{:S(2)}) copy-start(f32[32768,4]{0,1:T(4,128)} %convert_reduce_fusion.1) | copy-start | bytes 1572868
  310.6 15.6 %copy-start.9 = (f32[8192,16]{0,1:T(8,128)S(1)}, f32[8192,16]{0,1:T(8,128)}, u32[]{:S(2)}) copy-start(f32[8192,16]{0,1:T(8,128)} %copy-done.8) | copy-start | bytes 1572868
  310.6 15.6 %copy-start.14 = (f32[2,8,16,512]{3,1,2,0:T(8,128)S(1)}, f32[2,8,16,512]{3,1,2,0:T(8,128)}, u32[]{:S(2)}) copy-start(f32[2,8,16,512]{3,1,2,0:T(8,128)} %copy.68) | copy-start | bytes 1572868
  313.5 13.6 %copy-start.16 = (f32[1,16,16,512]{3,2,1,0:T(8,128)S(1)}, f32[1,16,16,512]{3,2,1,0:T(8,128)}, u32[]{:S(2)}) copy-start(f32[1,16,16,512]{3,2,1,0:T(8,128)} %get-tuple-element.54) | copy-start | bytes 1572868
  426.7 21.7 %copy-start.6 = (f32[3,16,16,512]{3,2,1,0:T(8,128)}, f32[3,16,16,512]{3,2,1,0:T(8,128)S(1)}, u32[]{:S(2)}) copy-start(f32[3,16,16,512]{3,2,1,0:T(8,128)S(1)} %all_to_all.41) | copy-start | bytes 4718596
  426.8 5.5 %collective-permute-start.12 = (f32[3,1,16,512]{3,2,1,0:T(8,128)S(1)}, f32[3,1,16,512]{3,2,1,0:T(8,128)S(1)}, u32[]{:S(2)}, u32[]{:S(2)}) collective-permute-start(f32[3,1,16,512]{3,2,1,0:T(8,128)S(1)} %get-tuple-element.56), channel_id=1, source_target_pairs={{0,4},{4,8},{8,12},{12,16},{16,20},{20,24},{24,28},{1,5},{5,9},{9,... | collective-permute-start | bytes 294920 | tf_op jit(solution)/shard_map/ppermute | solution.py:21
  430.3 6.8 %collective-permute-start.13 = (f32[3,1,16,512]{3,2,1,0:T(8,128)S(1)}, f32[3,1,16,512]{3,2,1,0:T(8,128)S(1)}, u32[]{:S(2)}, u32[]{:S(2)}) collective-permute-start(f32[3,1,16,512]{3,2,1,0:T(8,128)S(1)} %get-tuple-element.55), channel_id=1, source_target_pairs={{4,0},{8,4},{12,8},{16,12},{20,16},{24,20},{28,24},{5,1},{9,5},{13... | collective-permute-start | bytes 294920 | tf_op jit(solution)/shard_map/ppermute | solution.py:23
  437.4 5.9 %collective-permute-start.14 = (f32[3,18,1,512]{3,2,1,0:T(1,128)S(1)}, f32[3,18,1,512]{3,2,1,0:T(1,128)S(1)}, u32[]{:S(2)}, u32[]{:S(2)}) collective-permute-start(f32[3,18,1,512]{3,2,1,0:T(1,128)S(1)} %get-tuple-element.49), channel_id=1, source_target_pairs={{0,1},{1,2},{2,3},{4,5},{5,6},{6,7},{8,9},{9,10},{10,11},{12,13},{... | collective-permute-start | bytes 331784 | tf_op jit(solution)/shard_map/ppermute | solution.py:21
  441.2 5.5 %collective-permute-start.15 = (f32[3,18,1,512]{3,2,1,0:T(1,128)S(1)}, f32[3,18,1,512]{3,2,1,0:T(1,128)S(1)}, u32[]{:S(2)}, u32[]{:S(2)}) collective-permute-start(f32[3,18,1,512]{3,2,1,0:T(1,128)S(1)} %get-tuple-element.50), channel_id=1, source_target_pairs={{1,0},{2,1},{3,2},{5,4},{6,5},{7,6},{9,8},{10,9},{11,10},{13,12},{... | collective-permute-start | bytes 331784 | tf_op jit(solution)/shard_map/ppermute | solution.py:23
  448.5 1.0 copy-start.23
  448.7 1.8 copy-start.24
  450.5 1.0 copy-start.20
  451.5 1.1 copy-start.21
  451.5 1.7 copy-start.22
  452.6 1.2 copy-start.19
  454.5 1.7 copy-start.26
Sparse Core Ops, SparseCore 0:
  40.7 43.2 all-gather.4
  268.8 41.7 all-gather.6
